TPU v7x, 32 devices: a whole 2x2x4 slice. The times are simulated.
32 devices in a mesh: groups: 2 (over x), dom: 16 (over z, y, core).
Axes of the slice: x: 2, y: 2, z: 4, core: 2. Of those that a mesh axis runs over, the one named last changes fastest.
Arguments:
- node_feats: bfloat16 [32768, 256], P(('groups', 'dom')), parts along dimension 0, may hold values from -6 to 6
- tile_vals: bfloat16 [256, 24, 128, 128], P(('groups', 'dom')), parts along dimension 0, may hold values from 0 to 16, as said below
- tile_cols: int32 [256, 24], P(('groups', 'dom')), parts along dimension 0, may hold values from 0 to 127, as said below
- tile_count: int32 [256], P(('groups', 'dom')), parts along dimension 0, may hold values from 1 to 24, 1536 in all
- hist_cache: bfloat16 [2048, 256], P(('groups', 'dom')), parts along dimension 0, may hold values from -6 to 6
- bound_ids: int32 [256, 128], P(('groups', 'dom')), parts along dimension 0, may hold values from 0 to 1023, as said below
- bound_wts: bfloat16 [32768, 128], P(('groups', 'dom')), parts along dimension 0, may hold values from 0.049804688 to 1
- w_self: bfloat16 [256, 256], replicated, may hold values from -0.375 to 0.375
- w_neigh: bfloat16 [256, 256], replicated, may hold values from -6 to 6
- out_bias: float32 [256], replicated, may hold values from -3 to 3
- out_grad: bfloat16 [32768, 256], P(('groups', 'dom')), parts along dimension 0, may hold values from -6 to 6
Outputs:
- hidden_out: bfloat16 [32768, 256], P(('groups', 'dom')), parts along dimension 0
- feat_grad: bfloat16 [32768, 256], P(('groups', 'dom')), parts along dimension 0
- self_grad: float32 [512, 256], P('groups'), parts along dimension 0
- neigh_grad: float32 [512, 256], P('groups'), parts along dimension 0
- bias_grad: float32 [512], P('groups'), parts along dimension 0
There are 2 independent parts, one for each index of `groups`. A program takes and returns all parts, laid end to end along the dimension named above; an argument that names none is the same for every part. Nothing has to cross between parts.
Inputs may be any that keep to these rules, and one draw needn't show every extreme that they name: `tile_vals`: entries are zero or positive. `tile_cols`: entry s of row block b names a row block held by the device of b or by one of the two devices beside it on the closed loop of devices along dom; the 24 entries of a row block are distinct; only the first tile_count[b] are read. `tile_count`: one part's values sum to 1536. `bound_ids`: of the 1024 entries of one device's row blocks, at most 128 fall in the 64 rows of hist_cache held by any one device, and exactly 128 in those of some device.
All inputs are finite; a program needn't handle non-finite values. No bound on the sum of `tile_count` on one device may be relied on, other than what follows from the above.
Results may differ from a plain program's by a relative error of at most 0.0095.
Values may be sent and summed in bfloat16 or wider, within the bound.
A program may use at most 64 MiB of HBM per device.

v0:
```python
import math

import jax
import jax.numpy as jnp
from jax import lax
from jax.sharding import PartitionSpec as P


def padded(block, sides, width):
    for axis, dim in sides:
        count = lax.axis_size(axis)
        forward = [(i, i + 1) for i in range(count - 1)]
        forward.append((count - 1, 0))
        backward = [(target, source) for source, target in forward]
        low = lax.ppermute(
            lax.slice_in_dim(block, block.shape[dim] - width, None, axis=dim), axis, forward
        )
        high = lax.ppermute(lax.slice_in_dim(block, 0, width, axis=dim), axis, backward)
        block = jnp.concatenate([low, block, high], axis=dim)
    return block


def from_behind(value, axis, steps):
    count = lax.axis_size(axis)
    pairs = [(source, (source + steps) % count) for source in range(count)]
    return lax.ppermute(value, axis, pairs)


def band_slots(tile_cols, row_blocks, devices, device_index):
    owner_dev = tile_cols // row_blocks
    offset = jnp.mod(owner_dev - device_index + 1, devices)
    return offset * row_blocks + tile_cols % row_blocks


def body(
    node_feats,
    tile_vals,
    tile_cols,
    tile_count,
    hist_cache,
    bound_ids,
    bound_wts,
    w_self,
    w_neigh,
    out_bias,
    out_grad,
):
    row_blocks = tile_vals.shape[0]
    slot_count = tile_vals.shape[1]
    tile_size = tile_vals.shape[2]
    shard_rows = node_feats.shape[0]
    feat_width = node_feats.shape[1]
    bound_count = bound_ids.shape[1]
    devices = lax.axis_size("dom")
    device_index = lax.axis_index("dom")
    positions = band_slots(tile_cols, row_blocks, devices, device_index)
    live_mask = (jnp.arange(slot_count, dtype=jnp.int32)[None, :] < tile_count[:, None]).astype(
        jnp.float32
    )
    row_sums = jnp.sum(tile_vals, axis=3, dtype=jnp.float32)
    degrees = (
        1.0
        + jnp.einsum("bs,bsi->bi", live_mask, row_sums).reshape(shard_rows)
        + jnp.sum(bound_wts, axis=1, dtype=jnp.float32)
    )
    extended = padded(node_feats, (("dom", 0),), shard_rows)
    flat_ids = bound_ids.reshape(-1)
    whole_cache = lax.all_gather(hist_cache, "dom", axis=0, tiled=True)
    hist_rows = jnp.take(whole_cache, flat_ids, axis=0)
    hist_rows = hist_rows.reshape(row_blocks, bound_count, feat_width)
    hist_term = jnp.einsum(
        "rim,rmf->rif",
        bound_wts.reshape(row_blocks, tile_size, bound_count),
        hist_rows,
        preferred_element_type=jnp.float32,
    )
    band_hot = (
        positions[:, :, None] == jnp.arange(3 * row_blocks, dtype=jnp.int32)[None, None, :]
    ).astype(jnp.bfloat16) * live_mask[:, :, None].astype(jnp.bfloat16)
    band_matrix = (
        jnp.einsum("rsp,rsij->ripj", band_hot, tile_vals, preferred_element_type=jnp.float32)
        .astype(jnp.bfloat16)
        .reshape(shard_rows, 3 * shard_rows)
    )
    numerator = jnp.dot(band_matrix, extended, preferred_element_type=jnp.float32)
    numerator = numerator + hist_term.reshape(shard_rows, feat_width)
    aggregated = (numerator / degrees[:, None]).astype(jnp.bfloat16)
    pre_act = (
        jnp.dot(node_feats, w_self, preferred_element_type=jnp.float32)
        + jnp.dot(aggregated, w_neigh, preferred_element_type=jnp.float32)
        + out_bias[None, :]
    )
    sigmoid_of = jax.nn.sigmoid(pre_act)
    hidden_out = (pre_act * sigmoid_of).astype(jnp.bfloat16)
    dz_rows = (
        out_grad.astype(jnp.float32) * sigmoid_of * (1.0 + pre_act * (1.0 - sigmoid_of))
    ).astype(jnp.bfloat16)
    self_part = lax.dot_general(
        node_feats, dz_rows, (((0,), (0,)), ((), ())), preferred_element_type=jnp.float32
    )
    neigh_part = lax.dot_general(
        aggregated, dz_rows, (((0,), (0,)), ((), ())), preferred_element_type=jnp.float32
    )
    bias_part = jnp.sum(dz_rows, axis=0, dtype=jnp.float32)
    grad_sums = lax.psum((self_part, neigh_part, bias_part), "dom")
    inv_scale = 1.0 / math.sqrt(devices * shard_rows)
    back_neigh = lax.dot_general(
        dz_rows, w_neigh, (((1,), (1,)), ((), ())), preferred_element_type=jnp.float32
    )
    scaled = (back_neigh / degrees[:, None]).astype(jnp.bfloat16)
    partial_value = lax.dot_general(
        band_matrix, scaled, (((0,), (0,)), ((), ())), preferred_element_type=jnp.float32
    )
    from_right = from_behind(partial_value[:shard_rows], "dom", -1)
    from_left = from_behind(partial_value[2 * shard_rows :].astype(jnp.bfloat16), "dom", 1).astype(
        jnp.float32
    )
    neigh_total = partial_value[shard_rows : 2 * shard_rows] + from_right + from_left
    self_back = lax.dot_general(
        dz_rows, w_self, (((1,), (1,)), ((), ())), preferred_element_type=jnp.float32
    )
    feat_grad = (self_back + neigh_total).astype(jnp.bfloat16)
    return (
        hidden_out,
        feat_grad,
        grad_sums[0] * inv_scale,
        grad_sums[1] * inv_scale,
        grad_sums[2] * inv_scale,
    )


def solution(mesh):
    placed = (
        P(("groups", "dom"), None),
        P(("groups", "dom"), None, None, None),
        P(("groups", "dom"), None),
        P(("groups", "dom")),
        P(("groups", "dom"), None),
        P(("groups", "dom"), None),
        P(("groups", "dom"), None),
        P(),
        P(),
        P(),
        P(("groups", "dom"), None),
    )
    return jax.shard_map(
        body,
        mesh=mesh,
        in_specs=placed,
        out_specs=(
            P(("groups", "dom"), None),
            P(("groups", "dom"), None),
            P("groups", None),
            P("groups", None),
            P("groups"),
        ),
        check_vma=False,
    )
```

profile of v0, /device:TPU:0, one launch (start us, length us, event | category | flops | bytes accessed | tf_op | source)
XLA Modules:
  0.0 176.6 jit_solution(9752980473026221316)
XLA Ops:
  7.2 0.0 copy-start
  7.2 0.0 copy-start.2
  7.2 0.0 copy-start.6
  7.2 0.0 copy-start.5
  7.2 0.0 copy-start.7
  7.2 0.0 all-reduce.3.cloned.1.call-start
  7.3 5.5 %collective-permute-start.1 = (bf16[1024,256]{1,0:T(8,128)(2,1)}, bf16[1024,256]{1,0:T(8,128)(2,1)}, u32[]{:S(2)}, u32[]{:S(2)}) collective-permute-start(bf16[1024,256]{1,0:T(8,128)(2,1)} %param.11), channel_id=1, source_target_pairs={{1,0},{2,1},{3,2},{4,3},{5,4},{6,5},{7,6},{8,7},{9,8},{10,9},{11,1... | collective-permute-start | bytes 1572872 | tf_op jit(solution)/shard_map/ppermute | solution.py:18
  12.8 0.0 collective-permute-start
  12.8 0.7 compare_and_fusion
  13.5 0.7 fusion.48
  14.2 0.7 compare_select_fusion
  14.9 1.1 convert_reduce_fusion.2
  16.0 0.0 copy-start.3
  16.0 4.5 %convert_reduce_fusion = bf16[8,24,128]{2,1,0:T(8,128)(2,1)S(1)} fusion(bf16[8,24,128,128]{3,2,1,0:T(8,128)(2,1)} %param.12), kind=kLoop, calls=%fused_computation.1 | loop fusion | flops 6266880 | bytes 6340608 | tf_op jit(solution)/shard_map/reduce_sum | solution.py:60
  20.5 0.0 copy-done.6
  20.6 20.0 %all_gather.3 = bf16[1024,256]{1,0:T(8,128)(2,1)S(1)} all-gather(bf16[64,256]{1,0:T(8,128)(2,1)S(1)} %copy-done.6), channel_id=1, replica_groups=mesh['groups'=2,'dom'=16] {'dom'}, dimensions={0}, use_global_device_ids=true | all-gather | bytes 557056 | tf_op jit(solution)/shard_map/all_gather | solution.py:68
  40.6 0.0 copy-done.2
  40.6 0.0 copy-done.5
  40.6 0.3 fusion.53
  40.9 0.0 copy-done.7
  40.9 0.1 fusion.41
  41.0 3.9 %gather_fusion = bf16[1024,256]{1,0:T(8,128)(2,1)S(1)} fusion(bf16[1024,256]{1,0:T(8,128)(2,1)S(1)} %all_gather.3, s32[1024]{0:T(1024)S(1)} %broadcast_clamp_fusion), kind=kCustom, calls=%fused_computation | custom fusion | bytes 1052672 | tf_op jit(solution)/shard_map/jit(_take)/gather | solution.py:69
  45.0 0.0 copy-done.3
  45.0 0.4 fusion.31
  45.4 7.9 %fusion.8 = bf16[8,24,128,128]{3,1,2,0:T(8,128)(2,1)S(1)} fusion(bf16[8,24,128,128]{3,2,1,0:T(8,128)(2,1)} %param.12, s32[8,24]{1,0:T(8,128)S(1)} %fusion.47, bf16[8,24]{1,0:T(8,128)(2,1)S(1)} %get-tuple-element.16), kind=kOutput, calls=%fused_computation.10 | convolution fusion | flops 154149888 | bytes 12584064 | tf_op jit(solution)/shard_map/rsp,rsij->ripj/dot_general | solution.py:81
  53.3 0.0 collective-permute-done.1
  53.3 0.0 collective-permute-done
  53.3 0.0 copy-start.8
  53.3 0.0 copy-start.9
  53.3 3.9 %divide_convert_fusion = bf16[1024,256]{1,0:T(8,128)(2,1)S(1)} fusion(f32[1024,256]{1,0:T(8,128)S(1)} %bitcast.50, bf16[1024,256]{1,0:T(8,128)(2,1)} %collective-permute-done.1, bf16[1024,256]{1,0:T(8,128)(2,1)S(1)} %copy-done.2, bf16[1024,256]{1,0:T(8,128)(2,1)} %collective-permute-done, bf16[128,8,24,128]{3,2,1,0:T(8,128)(2,1)S(1)} %bitcast.46, ...), kind=kOutput, calls=%fused_computation.31 | convolution fusion | flops 1616117760 | bytes 9441280 | tf_op jit(solution)/shard_map/dot_general | solution.py:85
  57.3 1.5 convert_reduce_fusion.1
  58.8 6.9 %fusion = f32[3072,256]{1,0:T(8,128)} fusion(bf16[128,8,24,128]{3,2,1,0:T(8,128)(2,1)} %bitcast.47, bf16[1024,256]{1,0:T(8,128)(2,1)S(1)} %get-tuple-element.13, bf16[256,256]{1,0:T(8,128)(2,1)S(1)} %copy-done, f32[1024]{0:T(1024)S(1)} %bitcast_add_fusion), kind=kOutput, calls=%fused_computation.2 | convolution fusion | flops 1745354752 | bytes 10096640 | tf_op jit(solution)/shard_map/dot_general | solution.py:111
  65.7 1.3 slice.16
  66.9 0.9 collective-permute-start.2
  67.8 2.1 %slice.26 = bf16[1024,256]{1,0:T(8,128)(2,1)} slice(f32[3072,256]{1,0:T(8,128)} %fusion), slice={[2048:3072], [0:256]} | slice | bytes 1048576 | tf_op jit(solution)/shard_map/slice | solution.py:115
  69.9 0.0 collective-permute-start.3
  69.9 2.1 %fusion.54 = f32[256,256]{0,1:T(8,128)} fusion(bf16[1024,256]{1,0:T(8,128)(2,1)} %copy-done.4, bf16[1024,256]{1,0:T(8,128)(2,1)S(1)} %get-tuple-element.13), kind=kOutput, calls=%fused_computation.76 | convolution fusion | flops 134217728 | bytes 1310720 | tf_op jit(solution)/shard_map/dot_general | solution.py:101
  72.0 1.0 convolution_bitcast_fusion
  73.0 0.0 all-reduce.3.cloned.1.call-update
  73.0 37.3 %psum.23 = f32[256]{0:T(256)S(1)} all-reduce(f32[256]{0:T(256)S(1)} %get-tuple-element.12), channel_id=1, replica_groups=mesh['groups'=2,'dom'=16] {'dom'}, use_global_device_ids=true, to_apply=%region_5.6 | all-reduce | flops 256 | bytes 2048 | tf_op jit(solution)/shard_map/psum | solution.py:105
  110.3 0.6 broadcast_multiply_fusion.2
  110.9 53.6 %all-reduce.3.cloned.1.call-done = (f32[256,256]{0,1:T(8,128)}, f32[256,256]{0,1:T(8,128)}) async-done(((f32[256,256]{0,1:T(8,128)}, f32[256,256]{0,1:T(8,128)}), (f32[256,256]{0,1:T(8,128)}, f32[256,256]{0,1:T(8,128)})) %all-reduce.3.cloned.1.call-update) | async-done | bytes 524304 | tf_op jit(solution)/shard_map/psum | solution.py:105
  164.5 1.1 broadcast_multiply_fusion
  165.6 0.8 copy.19
  166.4 0.8 copy.18
  167.3 0.0 collective-permute-done.3
  167.3 0.0 collective-permute-done.2
  167.3 2.5 %fusion.25 = bf16[1024,256]{1,0:T(8,128)(2,1)} fusion(f32[1024,256]{1,0:T(8,128)S(1)} %collective-permute-done.2, f32[3072,256]{1,0:T(8,128)} %fusion, bf16[1024,256]{1,0:T(8,128)(2,1)} %collective-permute-done.3, bf16[1024,256]{1,0:T(8,128)(2,1)S(1)} %get-tuple-element.13, bf16[256,256]{1,0:T(8,128)(2,1)S(1)} %copy-done.5), kind=kOutput, calls=%fused_computation.26 | convolution fusion | flops 135528448 | bytes 3801088 | tf_op jit(solution)/shard_map/dot_general | solution.py:119
  (10 shorter events, 0.1 us)
Async XLA Ops:
  7.2 50.0 %copy-start = (bf16[256,256]{1,0:T(8,128)(2,1)S(1)}, bf16[256,256]{1,0:T(8,128)(2,1)}, u32[]{:S(2)}) copy-start(bf16[256,256]{1,0:T(8,128)(2,1)} %param.19) | copy-start | bytes 393220
  7.2 33.4 %copy-start.2 = (bf16[1024,256]{1,0:T(8,128)(2,1)S(1)}, bf16[1024,256]{1,0:T(8,128)(2,1)}, u32[]{:S(2)}) copy-start(bf16[1024,256]{1,0:T(8,128)(2,1)} %param.11) | copy-start | bytes 1572868
  7.2 13.4 %copy-start.6 = (bf16[64,256]{1,0:T(8,128)(2,1)S(1)}, bf16[64,256]{1,0:T(8,128)(2,1)}, u32[]{:S(2)}) copy-start(bf16[64,256]{1,0:T(8,128)(2,1)} %param.15) | copy-start | bytes 98308
  7.2 33.4 %copy-start.5 = (bf16[256,256]{1,0:T(8,128)(2,1)S(1)}, bf16[256,256]{1,0:T(8,128)(2,1)}, u32[]{:S(2)}) copy-start(bf16[256,256]{1,0:T(8,128)(2,1)} %param.18) | copy-start | bytes 393220
  7.2 33.7 %copy-start.7 = (s32[8,24]{1,0:T(8,128)S(1)}, s32[8,24]{1,0:T(8,128)}, u32[]{:S(2)}) copy-start(s32[8,24]{1,0:T(8,128)} %param.13) | copy-start | bytes 2308
  7.2 157.3 %all-reduce.3.cloned.1.call-start = ((), (), s32[]{:S(2)}) async-start(), calls=%async_computation | async-start | bytes 1048576 | tf_op jit(solution)/shard_map/psum | solution.py:105
  7.3 46.0 %collective-permute-start.1 = (bf16[1024,256]{1,0:T(8,128)(2,1)}, bf16[1024,256]{1,0:T(8,128)(2,1)}, u32[]{:S(2)}, u32[]{:S(2)}) collective-permute-start(bf16[1024,256]{1,0:T(8,128)(2,1)} %param.11), channel_id=1, source_target_pairs={{1,0},{2,1},{3,2},{4,3},{5,4},{6,5},{7,6},{8,7},{9,8},{10,9},{11,1... | collective-permute-start | bytes 1572872 | tf_op jit(solution)/shard_map/ppermute | solution.py:18
  12.8 40.5 %collective-permute-start = (bf16[1024,256]{1,0:T(8,128)(2,1)}, bf16[1024,256]{1,0:T(8,128)(2,1)}, u32[]{:S(2)}, u32[]{:S(2)}) collective-permute-start(bf16[1024,256]{1,0:T(8,128)(2,1)} %param.11), channel_id=1, source_target_pairs={{0,1},{1,2},{2,3},{3,4},{4,5},{5,6},{6,7},{7,8},{8,9},{9,10},{10,1... | collective-permute-start | bytes 1572872 | tf_op jit(solution)/shard_map/ppermute | solution.py:15
  16.0 29.0 %copy-start.3 = (bf16[1024,128]{1,0:T(8,128)(2,1)S(1)}, bf16[1024,128]{1,0:T(8,128)(2,1)}, u32[]{:S(2)}) copy-start(bf16[1024,128]{1,0:T(8,128)(2,1)} %param.17) | copy-start | bytes 786436
  53.3 4.0 %copy-start.1 = (bf16[8,24,128,128]{3,1,2,0:T(8,128)(2,1)}, bf16[8,24,128,128]{3,1,2,0:T(8,128)(2,1)S(1)}, u32[]{:S(2)}) copy-start(bf16[8,24,128,128]{3,1,2,0:T(8,128)(2,1)S(1)} %fusion.8) | copy-start | bytes 18874372
  53.3 3.9 %copy-start.8 = (bf16[1024,256]{1,0:T(8,128)(2,1)S(1)}, bf16[1024,256]{1,0:T(8,128)(2,1)}, u32[]{:S(2)}) copy-start(bf16[1024,256]{1,0:T(8,128)(2,1)} %param.21) | copy-start | bytes 1572868
  53.3 3.9 %copy-start.9 = (f32[256]{0:T(256)S(1)}, f32[256]{0:T(256)}, u32[]{:S(2)}) copy-start(f32[256]{0:T(256)} %param.20) | copy-start | bytes 3076
  57.2 1.5 copy-start.4
  66.9 100.3 %collective-permute-start.2 = (f32[1024,256]{1,0:T(8,128)S(1)}, f32[1024,256]{1,0:T(8,128)S(1)}, u32[]{:S(2)}, u32[]{:S(2)}) collective-permute-start(f32[1024,256]{1,0:T(8,128)S(1)} %slice.16), channel_id=1, source_target_pairs={{0,15},{1,0},{2,1},{3,2},{4,3},{5,4},{6,5},{7,6},{8,7},{9,8},{10,9... | collective-permute-start | bytes 3145736 | tf_op jit(solution)/shard_map/ppermute | solution.py:26
  69.9 97.4 %collective-permute-start.3 = (bf16[1024,256]{1,0:T(8,128)(2,1)}, bf16[1024,256]{1,0:T(8,128)(2,1)}, u32[]{:S(2)}, u32[]{:S(2)}) collective-permute-start(bf16[1024,256]{1,0:T(8,128)(2,1)} %slice.26), channel_id=1, source_target_pairs={{0,1},{1,2},{2,3},{3,4},{4,5},{5,6},{6,7},{7,8},{8,9},{9,10},{10,1... | collective-permute-start | bytes 1572872 | tf_op jit(solution)/shard_map/ppermute | solution.py:26
Sparse Core Ops, SparseCore 0:
  73.2 91.3 all-reduce.2
where the time goes:
time: 177 us
  blocking collectives  57.3 us (32%)
  waiting for transfers between devices  53.7 us (30%)
  matrix products  26.6 us (15%)
  between operations  14.2 us (8%)
  other arithmetic  9.42 us (5%)
  local copies, waits for them, and re-layouts  9.02 us (5%)
  starting transfers between devices  6.41 us (4%)
    psum x1, waiting for transfers between devices, body(): grad_sums = lax.psum((self_part, neigh_part, bias_part), 'dom')  53.6 us
    psum x1, blocking collectives, body(): grad_sums = lax.psum((self_part, neigh_part, bias_part), 'dom')  37.3 us
    all_gather x1, blocking collectives, body(): whole_cache = lax.all_gather(hist_cache, 'dom', axis=0, tiled=True)  20 us
    dot_general x1, matrix products, body(): jnp.einsum('rsp,rsij->ripj', band_hot, tile_vals, preferred_element_type=...  7.86 us
    dot_general x1, matrix products, body(): lax.dot_general(band_matrix, scaled, (((0,), (0,)), ((), ())), preferred_...  6.9 us
    ppermute x1, starting transfers between devices, padded(): lax.ppermute(lax.slice_in_dim(block, 0, width, axis=dim), axis, backward)  5.5 us
    reduce_sum x1, other arithmetic, body(): row_sums = jnp.sum(tile_vals, axis=3, dtype=jnp.float32)  4.55 us
    gather x1, local copies, waits for them, and re-layouts, body(): hist_rows = jnp.take(whole_cache, flat_ids, axis=0)  3.93 us
  transfers between devices with their start and end apart: 5, of which 1 were waited for; matrix products, arithmetic and copies ran while one was open for 16% of the time, Pallas kernels for 0%

commit v1 on v0

v1 whole, which is shorter than its diff:
```python
import functools
import math

import jax
import jax.numpy as jnp
from jax import lax
from jax.experimental import pallas as pl
from jax.experimental.pallas import tpu as pltpu
from jax.sharding import PartitionSpec as P

MESH = pl.DeviceIdType.MESH
F32 = jnp.float32
BF16 = jnp.bfloat16
NN = (((1,), (0,)), ((), ()))
NT = (((1,), (1,)), ((), ()))
TN = (((0,), (0,)), ((), ()))


def mm(a, b, dims):
    return lax.dot_general(a, b, dims, preferred_element_type=F32)


def layer_kernel(
    count,
    code_ref,
    ids_ref,
    wts_ref,
    ws_ref,
    wn_ref,
    bias_ref,
    og_ref,
    x_hbm,
    hist_hbm,
    tiles_hbm,
    hid_ref,
    feat_ref,
    gself_ref,
    gneigh_ref,
    gbias_ref,
    tiles,
    band,
    ext,
    rdeg,
    base,
    dz_s,
    agg_s,
    scaled_t,
    own_t,
    out_l,
    out_r,
    in_l,
    in_r,
    gsend,
    grecv,
    gfin,
    brow,
    local_sem,
    halo_sem,
    back_sem,
    hist_send,
    hist_recv,
    fwd_send,
    fwd_recv,
    rs_send,
    rs_recv,
    ag_send,
    ag_recv,
):
    rows = x_hbm.shape[0]
    feat = x_hbm.shape[1]
    row_blocks, slots, tile, _ = tiles.shape
    hrows = hist_hbm.shape[0]
    hist = count * hrows
    hbase = 3 * rows
    pairs = count // 2
    chunk = gfin.shape[1]
    inv_scale = 1.0 / math.sqrt(count * rows)

    me = lax.axis_index("dom")
    right = lax.rem(me + 1, count)
    left = lax.rem(me + count - 1, count)
    partner = me + 1 - 2 * lax.rem(me, 2)

    def remote(src, dst, send, recv, peer):
        return pltpu.make_async_remote_copy(
            src_ref=src,
            dst_ref=dst,
            send_sem=send,
            recv_sem=recv,
            device_id={"dom": peer},
            device_id_type=MESH,
        )

    barrier = pltpu.get_barrier_semaphore()

    @pl.loop(1, count)
    def _(d):
        pl.semaphore_signal(
            barrier, inc=1, device_id={"dom": lax.rem(me + d, count)}, device_id_type=MESH
        )

    own_rows = pl.ds(pl.multiple_of(hbase + me * hrows, hrows), hrows)
    tile_copy = pltpu.make_async_copy(tiles_hbm, tiles, local_sem.at[0])
    tile_copy.start()
    x_copy = pltpu.make_async_copy(x_hbm, ext.at[pl.ds(rows, rows)], local_sem.at[1])
    x_copy.start()
    h_copy = pltpu.make_async_copy(hist_hbm, ext.at[own_rows], local_sem.at[2])
    h_copy.start()

    pl.semaphore_wait(barrier, count - 1)

    def hist_copy(k):
        return remote(
            hist_hbm,
            ext.at[own_rows],
            hist_send.at[k],
            hist_recv.at[k],
            lax.rem(me + 2 * k, count),
        )

    def fwd_copy(k):
        src = lax.rem(me + count - 2 * k, count)
        at = pl.ds(pl.multiple_of(hbase + src * hrows, hrows), hrows)
        return remote(ext.at[at], ext.at[at], fwd_send.at[k], fwd_recv.at[k], partner)

    first = remote(hist_hbm, ext.at[own_rows], fwd_send.at[0], fwd_recv.at[0], partner)
    first.start()

    @pl.loop(1, pairs)
    def _(k):
        hist_copy(k).start()

    to_right = remote(
        x_hbm, ext.at[pl.ds(0, rows)], halo_sem.at[0], halo_sem.at[1], right
    )
    to_left = remote(
        x_hbm, ext.at[pl.ds(2 * rows, rows)], halo_sem.at[2], halo_sem.at[3], left
    )
    to_right.start()
    to_left.start()

    hstep = min(hist, 512)

    @pl.loop(0, row_blocks)
    def _(b):
        at = pl.ds(pl.multiple_of(b * tile, tile), tile)
        ids = ids_ref[pl.ds(b, 1), :]
        wts = wts_ref[at, :]
        for h in range(0, hist, hstep):
            hot = lax.broadcasted_iota(jnp.int32, (hstep, tile), 0) + h == ids
            hot = jnp.where(hot, 1.0, 0.0).astype(BF16)
            band[at, hbase + h : hbase + h + hstep] = mm(wts, hot, NT).astype(BF16)

    tile_copy.wait()
    x_copy.wait()
    h_copy.wait()

    @pl.loop(0, row_blocks)
    def _(b):
        at = pl.ds(pl.multiple_of(b * tile, tile), tile)
        total = wts_ref[at, :].astype(F32)
        for p in range(slots):
            code = code_ref[b, p]
            live = jnp.where(code >= 0, 1.0, 0.0)
            part = tiles[b, jnp.maximum(code, 0)].astype(F32) * live
            total = total + part
            band[at, p * tile : (p + 1) * tile] = part.astype(BF16)
        degree = 1.0 + jnp.sum(total, axis=1, keepdims=True)
        rdeg[at, :] = jnp.broadcast_to(1.0 / degree, (tile, feat))

    step = 256

    @pl.loop(1, pairs)
    def _(k):
        hist_copy(k).wait_recv()
        fwd_copy(k).start()

    @pl.loop(0, rows // step)
    def _(r):
        at = pl.ds(pl.multiple_of(r * step, step), step)
        base[at, :] = mm(band[at, rows : 2 * rows], ext[rows : 2 * rows, :], NN)

    first.wait_recv()

    @pl.loop(1, pairs)
    def _(k):
        fwd_copy(k).wait_recv()

    @pl.loop(0, rows // step)
    def _(r):
        at = pl.ds(pl.multiple_of(r * step, step), step)
        base[at, :] += mm(band[at, hbase:], ext[hbase:, :], NN)

    to_right.wait_recv()
    to_left.wait_recv()

    @pl.loop(0, rows // step)
    def _(r):
        at = pl.ds(pl.multiple_of(r * step, step), step)
        num = (
            base[at, :]
            + mm(band[at, :rows], ext[:rows, :], NN)
            + mm(band[at, 2 * rows : hbase], ext[2 * rows : hbase, :], NN)
        )
        recip = rdeg[at, :]
        agg = (num * recip).astype(BF16)
        x = ext[pl.ds(pl.multiple_of(rows + r * step, step), step), :]
        pre = mm(x, ws_ref[...], NN) + mm(agg, wn_ref[...], NN) + bias_ref[...]
        sig = jax.nn.sigmoid(pre)
        hid_ref[at, :] = (pre * sig).astype(BF16)
        dz = (og_ref[at, :].astype(F32) * sig * (1.0 + pre * (1.0 - sig))).astype(BF16)
        scaled = mm(dz, wn_ref[...], NT) * recip
        agg_s[at, :] = agg
        dz_s[at, :] = dz
        scaled_t[:, at] = scaled.T.astype(BF16)

    back_left = remote(out_l, in_r, back_sem.at[0], back_sem.at[1], left)
    back_right = remote(out_r, in_l, back_sem.at[2], back_sem.at[3], right)
    out_l[...] = mm(scaled_t[...], band[:, :rows], NN).astype(BF16)
    back_left.start()
    out_r[...] = mm(scaled_t[...], band[:, 2 * rows : hbase], NN).astype(BF16)
    back_right.start()

    dz = dz_s[...]
    bias_sum = jnp.sum(dz.astype(F32), axis=0, keepdims=True)
    high = bias_sum.astype(BF16).astype(F32)
    low = bias_sum - high
    row = lax.broadcasted_iota(jnp.int32, (16, 128), 0)
    zero = jnp.zeros((16, 128), F32)
    bias_rows = jnp.where(
        row == 0,
        high[:, :128],
        jnp.where(
            row == 1,
            high[:, 128:],
            jnp.where(row == 2, low[:, :128], jnp.where(row == 3, low[:, 128:], zero)),
        ),
    ).astype(BF16)
    grads = (mm(ext[rows : 2 * rows, :], dz, TN), mm(agg_s[...], dz, TN))
    for j in range(count):
        quarter, start = divmod(j * chunk, feat)
        half = (quarter % 2) * 128
        part = grads[quarter // 2][start : start + chunk, half : half + 128]
        gsend[j, :chunk, :] = part.astype(BF16)
        gsend[j, chunk:, :] = bias_rows

    def rs_copy(d):
        peer = lax.rem(me + d, count)
        return remote(gsend.at[peer], grecv.at[me], rs_send.at[d], rs_recv.at[d], peer)

    def ag_copy(d):
        peer = lax.rem(me + d, count)
        return remote(gfin.at[me], gfin.at[me], ag_send.at[d], ag_recv.at[d], peer)

    @pl.loop(1, count)
    def _(d):
        rs_copy(d).start()

    own_t[...] = mm(scaled_t[...], band[:, rows : 2 * rows], NN)

    @pl.loop(0, rows // step)
    def _(r):
        at = pl.ds(pl.multiple_of(r * step, step), step)
        base[at, :] = mm(dz_s[at, :], ws_ref[...], NT)

    @pl.loop(1, count)
    def _(d):
        rs_copy(d).wait_recv()

    def add(d, total):
        return total + grecv[lax.rem(me + d, count)].astype(F32)

    total = lax.fori_loop(1, count, add, gsend[me].astype(F32))
    gfin[me] = (total[:chunk] * inv_scale).astype(BF16)

    @pl.loop(1, count)
    def _(d):
        ag_copy(d).start()

    brow[...] = total[chunk:] * inv_scale
    gbias_ref[...] = brow[0:2, :] + brow[2:4, :]

    back_left.wait_recv()
    back_right.wait_recv()

    @pl.loop(0, rows // step)
    def _(r):
        at = pl.ds(pl.multiple_of(r * step, step), step)
        spread = own_t[:, at] + in_l[:, at].astype(F32) + in_r[:, at].astype(F32)
        feat_ref[at, :] = (base[at, :] + spread.T).astype(BF16)

    @pl.loop(1, count)
    def _(d):
        ag_copy(d).wait_recv()

    for j in range(count):
        quarter, start = divmod(j * chunk, feat)
        half = (quarter % 2) * 128
        out = gself_ref if quarter < 2 else gneigh_ref
        out[start : start + chunk, half : half + 128] = gfin[j].astype(F32)

    first.wait_send()
    to_right.wait_send()
    to_left.wait_send()
    back_left.wait_send()
    back_right.wait_send()

    @pl.loop(1, pairs)
    def _(k):
        hist_copy(k).wait_send()
        fwd_copy(k).wait_send()

    @pl.loop(1, count)
    def _(d):
        rs_copy(d).wait_send()
        ag_copy(d).wait_send()


def body(
    node_feats,
    tile_vals,
    tile_cols,
    tile_count,
    hist_cache,
    bound_ids,
    bound_wts,
    w_self,
    w_neigh,
    out_bias,
    out_grad,
):
    row_blocks, slots, tile, _ = tile_vals.shape
    rows, feat = node_feats.shape
    count = lax.axis_size("dom")
    me = lax.axis_index("dom")
    hist = count * hist_cache.shape[0]
    chunk = 2 * feat * feat // (128 * count)

    offset = jnp.mod(tile_cols // row_blocks - me + 1, count)
    positions = offset * row_blocks + tile_cols % row_blocks
    slot_ids = jnp.arange(slots, dtype=jnp.int32)
    here = (positions[:, :, None] == slot_ids[None, None, :]) & (
        slot_ids[None, :, None] < tile_count[:, None, None]
    )
    code = jnp.sum(jnp.where(here, slot_ids[None, :, None] + 1, 0), axis=1) - 1

    vmem = pl.BlockSpec(memory_space=pltpu.VMEM)
    anywhere = pl.BlockSpec(memory_space=pl.ANY)
    dma = pltpu.SemaphoreType.DMA
    outs = pl.pallas_call(
        functools.partial(layer_kernel, count),
        out_shape=(
            jax.ShapeDtypeStruct((rows, feat), BF16),
            jax.ShapeDtypeStruct((rows, feat), BF16),
            jax.ShapeDtypeStruct((feat, feat), F32),
            jax.ShapeDtypeStruct((feat, feat), F32),
            jax.ShapeDtypeStruct((2, feat // 2), F32),
        ),
        in_specs=[pl.BlockSpec(memory_space=pltpu.SMEM)] + [vmem] * 6 + [anywhere] * 3,
        out_specs=(vmem,) * 5,
        scratch_shapes=[
            pltpu.VMEM(tile_vals.shape, BF16),
            pltpu.VMEM((rows, 3 * rows + hist), BF16),
            pltpu.VMEM((3 * rows + hist, feat), BF16),
            pltpu.VMEM((rows, feat), F32),
            pltpu.VMEM((rows, feat), F32),
            pltpu.VMEM((rows, feat), BF16),
            pltpu.VMEM((rows, feat), BF16),
            pltpu.VMEM((feat, rows), BF16),
            pltpu.VMEM((feat, rows), F32),
            pltpu.VMEM((feat, rows), BF16),
            pltpu.VMEM((feat, rows), BF16),
            pltpu.VMEM((feat, rows), BF16),
            pltpu.VMEM((feat, rows), BF16),
            pltpu.VMEM((count, chunk + 16, 128), BF16),
            pltpu.VMEM((count, chunk + 16, 128), BF16),
            pltpu.VMEM((count, chunk, 128), BF16),
            pltpu.VMEM((16, 128), F32),
            dma((3,)),
            dma((4,)),
            dma((4,)),
            dma((count // 2,)),
            dma((count // 2,)),
            dma((count // 2,)),
            dma((count // 2,)),
            dma((count,)),
            dma((count,)),
            dma((count,)),
            dma((count,)),
        ],
        compiler_params=pltpu.CompilerParams(
            collective_id=0, has_side_effects=True, vmem_limit_bytes=56 * 1024 * 1024
        ),
    )(
        code,
        bound_ids,
        bound_wts,
        w_self,
        w_neigh,
        out_bias.reshape(1, feat),
        out_grad,
        node_feats,
        hist_cache,
        tile_vals,
    )
    return outs[:4] + (outs[4].reshape(feat),)


def solution(mesh):
    placed = (
        P(("groups", "dom"), None),
        P(("groups", "dom"), None, None, None),
        P(("groups", "dom"), None),
        P(("groups", "dom")),
        P(("groups", "dom"), None),
        P(("groups", "dom"), None),
        P(("groups", "dom"), None),
        P(),
        P(),
        P(),
        P(("groups", "dom"), None),
    )
    return jax.shard_map(
        body,
        mesh=mesh,
        in_specs=placed,
        out_specs=(
            P(("groups", "dom"), None),
            P(("groups", "dom"), None),
            P("groups", None),
            P("groups", None),
            P("groups"),
        ),
        check_vma=False,
    )
```

time: 177 us -> 62.6 us (0.35)
  blocking collectives: 57.3 us -> 0 us
  waiting for transfers between devices: 53.7 us -> 0 us
  Pallas kernels: 0 us -> 51.1 us
  matrix products: 26.6 us -> 0 us
  between operations: 14.2 us -> 0.66 us
  other arithmetic: 9.42 us -> 2.17 us
  starting transfers between devices: 6.41 us -> 0 us
    psum x1 -> x0, waiting for transfers between devices: 53.6 us -> none  [body(): grad_sums = lax.psum((self_part, neigh_part, bias_part), 'dom')]
    pallas_call x0 -> x1, Pallas kernels: none -> 51.1 us  [body(): pl.pallas_call(functools.partial(layer_kernel, count), out_shape=(jax.Sha...]
    psum x1 -> x0, blocking collectives: 37.3 us -> none  [body(): grad_sums = lax.psum((self_part, neigh_part, bias_part), 'dom')]
    dot_general x10 -> x0, matrix products: 26.6 us -> none  [the longest x1 7.86 us: body(): jnp.einsum('rsp,rsij->ripj', band_hot, tile_vals, preferred_element_type=...]
    all_gather x1 -> x0, blocking collectives: 20 us -> none  [body(): whole_cache = lax.all_gather(hist_cache, 'dom', axis=0, tiled=True)]
    unnamed x22 -> x5, local copies, waits for them, and re-layouts: 1.73 us -> 8.3 us
    ppermute x4 -> x0, starting transfers between devices: 6.37 us -> none  [the longest x1 5.5 us: padded(): lax.ppermute(lax.slice_in_dim(block, 0, width, axis=dim), axis, backward)]
    reduce_sum x2 -> x1, other arithmetic: 5.64 us -> 0.13 us  [body(): code = jnp.sum(jnp.where(here, slot_ids[None, :, None] + 1, 0), axis=1) - 1]
  transfers between devices with their start and end apart: 5 -> 0, of which waited for: 1 -> 0; matrix products, arithmetic and copies ran while one was open for 16% -> 0% of each run, Pallas kernels for 0% -> 0%
where the time goes in v1:
time: 62.6 us; the launch traced here: 62.3 us
  Pallas kernels  51.1 us (82%)
  local copies, waits for them, and re-layouts  8.3 us (13%)
  other arithmetic  2.17 us (3%)
  between operations  0.66 us (1%)
    pallas_call x1, Pallas kernels, body(): pl.pallas_call(functools.partial(layer_kernel, count), out_shape=(jax.Sha...  51.1 us
    unnamed x5, local copies, waits for them, and re-layouts  8.3 us

profile of v1, /device:TPU:0, one launch (start us, length us, event | category | flops | bytes accessed | tf_op | source)
XLA Modules:
  0.0 62.3 jit_solution(10465049411393030271)
XLA Ops:
  0.6 0.7 %iota_compare_fusion.1 = pred[8,24]{1,0:T(8,128)(4,1)S(1)} fusion(s32[8]{0:T(128)} %param.14), kind=kLoop, calls=%fused_computation.16 | loop fusion | flops 192 | bytes 224 | tf_op jit(solution)/shard_map/lt | solution.py:343
  1.4 0.7 %fusion.5 = s32[8,24]{1,0:T(8,128)S(1)} fusion(s32[8,24]{1,0:T(8,128)} %param.13, s32[]{:T(128)S(6)} %axis_index.12), kind=kLoop, calls=%fused_computation.15 | loop fusion | flops 6528 | bytes 1540 | tf_op jit(solution)/shard_map/add | solution.py:340
  2.1 0.1 select_reduce_fusion
  2.2 0.6 broadcast_add_fusion.code_ref
  2.8 51.1 %shard_map.146 = (bf16[1024,256]{1,0:T(8,128)(2,1)}, bf16[1024,256]{1,0:T(8,128)(2,1)}, f32[256,256]{1,0:T(8,128)}, f32[256,256]{1,0:T(8,128)}, f32[2,128]{1,0:T(2,128)}) custom-call(s32[8,24]{1,0:T(8,128)} %broadcast_add_fusion.code_ref, s32[8,128]{1,0:T(8,128)} %ids_ref.1, bf16[1024,128]{1,0:T(8,128)(2,1)} %wts_ref.1, bf16[256,256]{1,0:T(8,128)(2,1)} %ws_ref.1, ...), custom_call_target="tpu_custom_call" | custom-call | tf_op jit(solution)/shard_map/pallas_call | solution.py:350
  54.0 1.9 %copy.21 = bf16[1024,256]{1,0:T(8,128)(2,1)} copy(bf16[1024,256]{1,0:T(8,128)(2,1)} %get-tuple-element.20) | data formatting | bytes 1048576
  55.8 1.9 %copy.22 = bf16[1024,256]{1,0:T(8,128)(2,1)} copy(bf16[1024,256]{1,0:T(8,128)(2,1)} %get-tuple-element.21) | data formatting | bytes 1048576
  57.7 1.7 %copy.23 = f32[256,256]{1,0:T(8,128)} copy(f32[256,256]{1,0:T(8,128)} %get-tuple-element.22) | data formatting | bytes 524288
  59.4 1.7 %copy.24 = f32[256,256]{1,0:T(8,128)} copy(f32[256,256]{1,0:T(8,128)} %get-tuple-element.23) | data formatting | bytes 524288
  61.0 1.2 %copy.25 = f32[256]{0:T(256)} copy(f32[256]{0:T(256)} %bitcast.3) | data formatting | bytes 2048
  (1 shorter events, 0.0 us)

commit v2 on v1

v2 whole, which is shorter than its diff:
```python
import functools
import math

import jax
import jax.numpy as jnp
from jax import lax
from jax.experimental import pallas as pl
from jax.experimental.pallas import tpu as pltpu
from jax.sharding import PartitionSpec as P

MESH = pl.DeviceIdType.MESH
F32 = jnp.float32
BF16 = jnp.bfloat16
NN = (((1,), (0,)), ((), ()))
NT = (((1,), (1,)), ((), ()))
TN = (((0,), (0,)), ((), ()))


def mm(a, b, dims):
    return lax.dot_general(a, b, dims, preferred_element_type=F32)


def layer_kernel(
    count,
    live_ref,
    cols_ref,
    ids_ref,
    bias_ref,
    wts_hbm,
    ws_hbm,
    wn_hbm,
    og_hbm,
    x_hbm,
    hist_hbm,
    tiles_hbm,
    hid_ref,
    feat_ref,
    gself_ref,
    gneigh_ref,
    gbias_ref,
    wts_ref,
    ws_ref,
    wn_ref,
    og_ref,
    tiles,
    band,
    ext,
    rdeg,
    base,
    pre_s,
    dz_s,
    agg_s,
    scaled_t,
    own_t,
    out_far,
    out_near,
    in_far,
    in_near,
    gsend,
    gpair,
    gsum,
    grecv,
    gfin,
    brow,
    code_vec,
    code_ref,
    local_sem,
    halo_send,
    halo_recv,
    back_send,
    back_recv,
    hist_send,
    hist_recv,
    fwd_send,
    fwd_recv,
    pair_sem,
    rs_send,
    rs_recv,
    ag_send,
    ag_recv,
    agf_send,
    agf_recv,
):
    rows = x_hbm.shape[0]
    feat = x_hbm.shape[1]
    row_blocks, slots, tile, _ = tiles.shape
    hrows = hist_hbm.shape[0]
    hist = count * hrows
    hbase = 3 * rows
    pairs = count // 2
    chunk = gfin.shape[1]
    inv_scale = 1.0 / math.sqrt(count * rows)
    step = 256
    half = rows // 2

    me = lax.axis_index("dom")
    side = lax.rem(me, 2)
    partner = me + 1 - 2 * side
    far = lax.rem(me + count - 1 + 2 * side, count)

    def peer_of(k):
        return lax.rem(me + 2 * k, count)

    def source_of(k):
        return lax.rem(me + count - 2 * k, count)

    def remote(src, dst, send, recv, peer):
        return pltpu.make_async_remote_copy(
            src_ref=src,
            dst_ref=dst,
            send_sem=send,
            recv_sem=recv,
            device_id={"dom": peer},
            device_id_type=MESH,
        )

    def greet(peer):
        pl.semaphore_signal(barrier, inc=1, device_id={"dom": peer}, device_id_type=MESH)

    barrier = pltpu.get_barrier_semaphore()
    greet(far)
    greet(partner)

    @pl.loop(1, pairs)
    def _(k):
        greet(peer_of(k))

    own_rows = pl.ds(pl.multiple_of(hbase + me * hrows, hrows), hrows)
    pieces = (
        (wts_hbm, wts_ref),
        (hist_hbm, ext.at[own_rows]),
        (x_hbm, ext.at[pl.ds(rows, rows)]),
        (ws_hbm, ws_ref),
        (wn_hbm, wn_ref),
        (tiles_hbm, tiles),
        (og_hbm, og_ref),
    )
    loads = [pltpu.make_async_copy(a, b, local_sem.at[i]) for i, (a, b) in enumerate(pieces)]
    for load in loads:
        load.start()

    pl.semaphore_wait(barrier, pairs + 1)

    far_there = (1 - side) * 2 * rows
    near_there = side * 2 * rows
    far_here = side * 2 * rows
    near_here = (1 - side) * 2 * rows

    def halo_far(j):
        at = pl.ds(pl.multiple_of(far_there + j * half, half), half)
        return remote(
            x_hbm.at[pl.ds(j * half, half)], ext.at[at], halo_send.at[j], halo_recv.at[j], far
        )

    halo_near = remote(
        x_hbm,
        ext.at[pl.ds(pl.multiple_of(near_there, rows), rows)],
        halo_send.at[2],
        halo_recv.at[2],
        partner,
    )

    def hist_copy(k):
        return remote(
            hist_hbm, ext.at[own_rows], hist_send.at[k], hist_recv.at[k], peer_of(k)
        )

    def fwd_copy(k):
        at = pl.ds(pl.multiple_of(hbase + source_of(k) * hrows, hrows), hrows)
        return remote(ext.at[at], ext.at[at], fwd_send.at[k], fwd_recv.at[k], partner)

    first = remote(hist_hbm, ext.at[own_rows], fwd_send.at[0], fwd_recv.at[0], partner)

    @pl.loop(1, pairs)
    def _(k):
        hist_copy(k).start()

    halo_far(0).start()
    halo_far(1).start()
    first.start()
    halo_near.start()

    blocks = count * row_blocks
    pos = cols_ref[...] - (me - 1) * row_blocks
    pos = jnp.where(pos < 0, pos + blocks, jnp.where(pos >= blocks, pos - blocks, pos))
    block_of = lax.broadcasted_iota(jnp.int32, code_vec.shape, 0)
    place = lax.broadcasted_iota(jnp.int32, code_vec.shape, 1)
    limit = jnp.zeros(code_vec.shape, jnp.int32)
    for b in range(row_blocks):
        limit = jnp.where(block_of == b, live_ref[b], limit)
    code = jnp.full(code_vec.shape, -1, jnp.int32)
    for s in range(slots):
        code = jnp.where((pos[:, s : s + 1] == place) & (limit > s), s, code)
    code_vec[...] = code
    code_copy = pltpu.make_async_copy(code_vec, code_ref, local_sem.at[len(pieces)])
    code_copy.start()

    hstep = min(hist, 512)
    loads[0].wait()

    @pl.loop(0, row_blocks)
    def _(b):
        at = pl.ds(pl.multiple_of(b * tile, tile), tile)
        ids = ids_ref[pl.ds(b, 1), :]
        wts = wts_ref[at, :]
        for h in range(0, hist, hstep):
            hot = lax.broadcasted_iota(jnp.int32, (hstep, tile), 0) + h == ids
            hot = jnp.where(hot, 1.0, 0.0).astype(BF16)
            band[at, hbase + h : hbase + h + hstep] = mm(wts, hot, NT).astype(BF16)

    for load in loads[1:]:
        load.wait()
    code_copy.wait()

    @pl.loop(0, row_blocks)
    def _(b):
        at = pl.ds(pl.multiple_of(b * tile, tile), tile)
        total = wts_ref[at, :].astype(F32)
        for p in range(slots):
            code = code_ref[b, p]
            live = jnp.where(code >= 0, 1.0, 0.0)
            part = tiles[b, jnp.maximum(code, 0)].astype(F32) * live
            total = total + part
            band[at, p * tile : (p + 1) * tile] = part.astype(BF16)
        degree = 1.0 + jnp.sum(total, axis=1, keepdims=True)
        rdeg[at, :] = jnp.broadcast_to(1.0 / degree, (tile, feat))

    @pl.loop(1, pairs)
    def _(k):
        hist_copy(k).wait_recv()
        fwd_copy(k).start()

    @pl.loop(0, rows // step)
    def _(r):
        at = pl.ds(pl.multiple_of(r * step, step), step)
        own = ext[pl.ds(pl.multiple_of(rows + r * step, step), step), :]
        base[at, :] = mm(band[at, rows : 2 * rows], ext[rows : 2 * rows, :], NN)
        pre_s[at, :] = mm(own, ws_ref[...], NN) + bias_ref[...]

    halo_near.wait_recv()
    first.wait_recv()

    @pl.loop(1, pairs)
    def _(k):
        fwd_copy(k).wait_recv()

    near_at = pl.ds(pl.multiple_of(near_here, rows), rows)
    far_at = pl.ds(pl.multiple_of(far_here, rows), rows)
    far_half = [pl.ds(pl.multiple_of(far_here + j * half, half), half) for j in range(2)]

    @pl.loop(0, rows // step)
    def _(r):
        at = pl.ds(pl.multiple_of(r * step, step), step)
        base[at, :] += mm(band[at, hbase:], ext[hbase:, :], NN) + mm(
            band[at, near_at], ext[near_at, :], NN
        )

    halo_far(0).wait_recv()

    @pl.loop(0, rows // step)
    def _(r):
        at = pl.ds(pl.multiple_of(r * step, step), step)
        base[at, :] += mm(band[at, far_half[0]], ext[far_half[0], :], NN)

    halo_far(1).wait_recv()

    @pl.loop(0, rows // step)
    def _(r):
        at = pl.ds(pl.multiple_of(r * step, step), step)
        num = base[at, :] + mm(band[at, far_half[1]], ext[far_half[1], :], NN)
        recip = rdeg[at, :]
        agg = (num * recip).astype(BF16)
        pre = pre_s[at, :] + mm(agg, wn_ref[...], NN)
        sig = jax.nn.sigmoid(pre)
        hid_ref[at, :] = (pre * sig).astype(BF16)
        dz = (og_ref[at, :].astype(F32) * sig * (1.0 + pre * (1.0 - sig))).astype(BF16)
        scaled = mm(dz, wn_ref[...], NT) * recip
        agg_s[at, :] = agg
        dz_s[at, :] = dz
        scaled_t[:, at] = scaled.T.astype(BF16)

    dz = dz_s[...]
    bias_sum = jnp.sum(dz.astype(F32), axis=0, keepdims=True)
    row = lax.broadcasted_iota(jnp.int32, (16, 128), 0)
    bias_rows = jnp.where(
        row == 0, bias_sum[:, :128], jnp.where(row == 1, bias_sum[:, 128:], 0.0)
    ).astype(BF16)
    grads = (mm(ext[rows : 2 * rows, :], dz, TN), mm(agg_s[...], dz, TN))
    for j in range(count):
        quarter, start = divmod(j * chunk, feat)
        lanes = (quarter % 2) * 128
        part = grads[quarter // 2][start : start + chunk, lanes : lanes + 128]
        gsend[j % 2, j // 2, :chunk, :] = part.astype(BF16)
        gsend[j % 2, j // 2, chunk:, :] = bias_rows

    pair_copy = remote(gsend.at[1 - side], gpair, pair_sem.at[0], pair_sem.at[1], partner)
    pair_copy.start()

    back_far = remote(out_far, in_far, back_send.at[0], back_recv.at[0], far)
    back_near = remote(out_near, in_near, back_send.at[1], back_recv.at[1], partner)
    out_far[...] = mm(scaled_t[...], band[:, far_at], NN).astype(BF16)
    back_far.start()

    chip = me // 2

    def rs_copy(k):
        peer = peer_of(k)
        return remote(
            gsum.at[peer // 2], grecv.at[chip], rs_send.at[k], rs_recv.at[k], peer
        )

    def ag_copy(k):
        return remote(gfin.at[me], gfin.at[me], ag_send.at[k], ag_recv.at[k], peer_of(k))

    def agf_copy(k):
        src = source_of(k)
        return remote(gfin.at[src], gfin.at[src], agf_send.at[k], agf_recv.at[k], partner)

    pair_copy.wait_recv()
    gsum[...] = (gsend[side].astype(F32) + gpair[...].astype(F32)).astype(BF16)

    @pl.loop(1, pairs)
    def _(k):
        rs_copy(k).start()

    out_near[...] = mm(scaled_t[...], band[:, near_at], NN).astype(BF16)
    back_near.start()
    own_t[...] = mm(scaled_t[...], band[:, rows : 2 * rows], NN)

    @pl.loop(0, rows // step)
    def _(r):
        at = pl.ds(pl.multiple_of(r * step, step), step)
        base[at, :] = mm(dz_s[at, :], ws_ref[...], NT)

    @pl.loop(1, pairs)
    def _(k):
        rs_copy(k).wait_recv()

    def add(k, total):
        return total + grecv[lax.rem(chip + k, pairs)].astype(F32)

    total = lax.fori_loop(1, pairs, add, gsum[chip].astype(F32))
    gfin[me] = (total[:chunk] * inv_scale).astype(BF16)
    agf_first = agf_copy(0)
    agf_first.start()

    @pl.loop(1, pairs)
    def _(k):
        ag_copy(k).start()

    brow[...] = total[chunk:] * inv_scale
    gbias_ref[...] = brow[0:2, :]

    @pl.loop(1, pairs)
    def _(k):
        ag_copy(k).wait_recv()
        agf_copy(k).start()

    back_near.wait_recv()
    back_far.wait_recv()

    @pl.loop(0, rows // step)
    def _(r):
        at = pl.ds(pl.multiple_of(r * step, step), step)
        spread = own_t[:, at] + in_near[:, at].astype(F32) + in_far[:, at].astype(F32)
        feat_ref[at, :] = (base[at, :] + spread.T).astype(BF16)

    agf_first.wait_recv()

    @pl.loop(1, pairs)
    def _(k):
        agf_copy(k).wait_recv()

    for j in range(count):
        quarter, start = divmod(j * chunk, feat)
        lanes = (quarter % 2) * 128
        out = gself_ref if quarter < 2 else gneigh_ref
        out[start : start + chunk, lanes : lanes + 128] = gfin[j].astype(F32)

    first.wait_send()
    halo_far(0).wait_send()
    halo_far(1).wait_send()
    halo_near.wait_send()
    back_far.wait_send()
    back_near.wait_send()
    pair_copy.wait_send()
    agf_first.wait_send()

    @pl.loop(1, pairs)
    def _(k):
        hist_copy(k).wait_send()
        fwd_copy(k).wait_send()
        rs_copy(k).wait_send()
        ag_copy(k).wait_send()
        agf_copy(k).wait_send()


def hand_over(count, *refs):
    given, taken, held = refs[:count], refs[count : 2 * count], refs[2 * count : 3 * count]
    sems = refs[-1]
    into = [pltpu.make_async_copy(given[i], held[i], sems.at[0, i]) for i in range(count)]
    out = [pltpu.make_async_copy(held[i], taken[i], sems.at[1, i]) for i in range(count)]
    for copy in into:
        copy.start()
    for i in range(count):
        into[i].wait()
        out[i].start()
    for copy in out:
        copy.wait()


def body(
    node_feats,
    tile_vals,
    tile_cols,
    tile_count,
    hist_cache,
    bound_ids,
    bound_wts,
    w_self,
    w_neigh,
    out_bias,
    out_grad,
):
    row_blocks, slots, tile, _ = tile_vals.shape
    rows, feat = node_feats.shape
    count = lax.axis_size("dom")
    pairs = count // 2
    hist = count * hist_cache.shape[0]
    chunk = 2 * feat * feat // (128 * count)

    vmem = pl.BlockSpec(memory_space=pltpu.VMEM)
    anywhere = pl.BlockSpec(memory_space=pl.ANY)
    dma = pltpu.SemaphoreType.DMA
    outs = pl.pallas_call(
        functools.partial(layer_kernel, count),
        out_shape=(
            jax.ShapeDtypeStruct((rows, feat), BF16),
            jax.ShapeDtypeStruct((rows, feat), BF16),
            jax.ShapeDtypeStruct((feat, feat), F32),
            jax.ShapeDtypeStruct((feat, feat), F32),
            jax.ShapeDtypeStruct((2, feat // 2), F32),
        ),
        in_specs=[pl.BlockSpec(memory_space=pltpu.SMEM)] + [vmem] * 3 + [anywhere] * 7,
        out_specs=(vmem,) * 5,
        scratch_shapes=[
            pltpu.VMEM(bound_wts.shape, BF16),
            pltpu.VMEM((feat, feat), BF16),
            pltpu.VMEM((feat, feat), BF16),
            pltpu.VMEM((rows, feat), BF16),
            pltpu.VMEM(tile_vals.shape, BF16),
            pltpu.VMEM((rows, 3 * rows + hist), BF16),
            pltpu.VMEM((3 * rows + hist, feat), BF16),
            pltpu.VMEM((rows, feat), F32),
            pltpu.VMEM((rows, feat), F32),
            pltpu.VMEM((rows, feat), F32),
            pltpu.VMEM((rows, feat), BF16),
            pltpu.VMEM((rows, feat), BF16),
            pltpu.VMEM((feat, rows), BF16),
            pltpu.VMEM((feat, rows), F32),
            pltpu.VMEM((feat, rows), BF16),
            pltpu.VMEM((feat, rows), BF16),
            pltpu.VMEM((feat, rows), BF16),
            pltpu.VMEM((feat, rows), BF16),
            pltpu.VMEM((2, pairs, chunk + 16, 128), BF16),
            pltpu.VMEM((pairs, chunk + 16, 128), BF16),
            pltpu.VMEM((pairs, chunk + 16, 128), BF16),
            pltpu.VMEM((pairs, chunk + 16, 128), BF16),
            pltpu.VMEM((count, chunk, 128), BF16),
            pltpu.VMEM((16, 128), F32),
            pltpu.VMEM((row_blocks, 128), jnp.int32),
            pltpu.SMEM((row_blocks, 128), jnp.int32),
            dma((8,)),
            dma((3,)),
            dma((3,)),
            dma((2,)),
            dma((2,)),
            dma((pairs,)),
            dma((pairs,)),
            dma((pairs,)),
            dma((pairs,)),
            dma((2,)),
            dma((pairs,)),
            dma((pairs,)),
            dma((pairs,)),
            dma((pairs,)),
            dma((pairs,)),
            dma((pairs,)),
        ],
        compiler_params=pltpu.CompilerParams(
            collective_id=0, has_side_effects=True, vmem_limit_bytes=56 * 1024 * 1024
        ),
    )(
        tile_count,
        tile_cols,
        bound_ids,
        out_bias.reshape(1, feat),
        bound_wts,
        w_self,
        w_neigh,
        out_grad,
        node_feats,
        hist_cache,
        tile_vals,
    )
    outs = pl.pallas_call(
        functools.partial(hand_over, 5),
        out_shape=tuple(jax.ShapeDtypeStruct(o.shape, o.dtype) for o in outs),
        in_specs=[anywhere] * 5,
        out_specs=(anywhere,) * 5,
        scratch_shapes=[pltpu.VMEM(o.shape, o.dtype) for o in outs] + [dma((2, 5))],
        compiler_params=pltpu.CompilerParams(vmem_limit_bytes=56 * 1024 * 1024),
    )(*outs)
    return outs[:4] + (outs[4].reshape(feat),)


def solution(mesh):
    placed = (
        P(("groups", "dom"), None),
        P(("groups", "dom"), None, None, None),
        P(("groups", "dom"), None),
        P(("groups", "dom")),
        P(("groups", "dom"), None),
        P(("groups", "dom"), None),
        P(("groups", "dom"), None),
        P(),
        P(),
        P(),
        P(("groups", "dom"), None),
    )
    return jax.shard_map(
        body,
        mesh=mesh,
        in_specs=placed,
        out_specs=(
            P(("groups", "dom"), None),
            P(("groups", "dom"), None),
            P("groups", None),
            P("groups", None),
            P("groups"),
        ),
        check_vma=False,
    )
```

time: 62.6 us -> 50.5 us (0.81)
  local copies, waits for them, and re-layouts: 8.3 us -> 0 us
  other arithmetic: 2.17 us -> 0 us
  Pallas kernels: 51.1 us -> 49.7 us
    unnamed x5 -> x0, local copies, waits for them, and re-layouts: 8.3 us -> none
    pallas_call x1, Pallas kernels: 51.1 us -> 47.4 us  [body(): pl.pallas_call(functools.partial(layer_kernel, count), out_shape=(jax.Sha...]
    pallas_call x0 -> x1, Pallas kernels: none -> 2.27 us  [body(): pl.pallas_call(functools.partial(hand_over, 5), out_shape=tuple((jax.Shap...]
    lt x1 -> x0, other arithmetic: 0.73 us -> none  [body(): slot_ids[None, :, None] < tile_count[:, None, None]]
    add x2 -> x0, other arithmetic: 0.71 us -> none  [the longest x1 0.71 us: body(): positions = offset * row_blocks + tile_cols % row_blocks]
where the time goes in v2:
time: 50.5 us; the launch traced here: 50.3 us
  Pallas kernels  49.7 us (98%)
  between operations  0.64 us (1%)
    pallas_call x1, Pallas kernels, body(): pl.pallas_call(functools.partial(layer_kernel, count), out_shape=(jax.Sha...  47.4 us
    pallas_call x1, Pallas kernels, body(): pl.pallas_call(functools.partial(hand_over, 5), out_shape=tuple((jax.Shap...  2.27 us

profile of v2, /device:TPU:0, one launch (start us, length us, event | category | flops | bytes accessed | tf_op | source)
XLA Modules:
  0.0 50.3 jit_solution(6758205348985258384)
XLA Ops:
  0.6 47.4 %shard_map.146 = (bf16[1024,256]{1,0:T(8,128)(2,1)}, bf16[1024,256]{1,0:T(8,128)(2,1)}, f32[256,256]{1,0:T(8,128)}, f32[256,256]{1,0:T(8,128)}, f32[2,128]{1,0:T(2,128)}) custom-call(s32[8]{0:T(128)} %live_ref.1, s32[8,24]{1,0:T(8,128)} %cols_ref.1, s32[8,128]{1,0:T(8,128)} %ids_ref.1, f32[1,256]{1,0:T(1,128)} %bitcast.2, bf16[1024,128]{1,0:T(8,128)(2,1)} %wts_hbm.1, ...), custom_call_target="tpu_custom_call" | custom-call | tf_op jit(solution)/shard_map/pallas_call | solution.py:435
  48.1 2.3 %shard_map.147 = (bf16[1024,256]{1,0:T(8,128)(2,1)}, bf16[1024,256]{1,0:T(8,128)(2,1)}, f32[256,256]{1,0:T(8,128)}, f32[256,256]{1,0:T(8,128)}, f32[2,128]{1,0:T(2,128)}) custom-call(bf16[1024,256]{1,0:T(8,128)(2,1)} %get-tuple-element.15.refs_0_, bf16[1024,256]{1,0:T(8,128)(2,1)} %get-tuple-element.16.refs_1_, f32[256,256]{1,0:T(8,128)} %get-tuple-element.17.refs_2_, ...), custom_call_target="tpu_custom_call" | custom-call | tf_op jit(solution)/shard_map/pallas_call | solution.py:506

commit v3 on v2

--- a/solution.py
+++ b/solution.py
@@ -13,7 +13,6 @@
 BF16 = jnp.bfloat16
 NN = (((1,), (0,)), ((), ()))
 NT = (((1,), (1,)), ((), ()))
-TN = (((0,), (0,)), ((), ()))
 
 
 def mm(a, b, dims):
@@ -49,7 +48,8 @@
     base,
     pre_s,
     dz_s,
-    agg_s,
+    x_t,
+    agg_t,
     scaled_t,
     own_t,
     out_far,
@@ -160,24 +160,33 @@
         partner,
     )
 
-    def hist_copy(k):
+    quads = count // 4
+    twin = me + 2 - 4 * lax.rem(me // 2, 2)
+
+    def shard(i):
+        return ext.at[pl.ds(pl.multiple_of(hbase + i * hrows, hrows), hrows)]
+
+    def hop(owner, k, slot):
         return remote(
-            hist_hbm, ext.at[own_rows], hist_send.at[k], hist_recv.at[k], peer_of(k)
+            shard(owner), shard(owner), hist_send.at[slot], hist_recv.at[slot], peer_of(2 * k)
         )
 
-    def fwd_copy(k):
-        at = pl.ds(pl.multiple_of(hbase + source_of(k) * hrows, hrows), hrows)
-        return remote(ext.at[at], ext.at[at], fwd_send.at[k], fwd_recv.at[k], partner)
-
-    first = remote(hist_hbm, ext.at[own_rows], fwd_send.at[0], fwd_recv.at[0], partner)
-
-    @pl.loop(1, pairs)
-    def _(k):
-        hist_copy(k).start()
+    def fwd_copy(slot):
+        second = slot // quads
+        src = source_of(2 * lax.rem(slot, quads))
+        src = src + second * (2 - 4 * lax.rem(me // 2, 2))
+        return remote(shard(src), shard(src), fwd_send.at[slot], fwd_recv.at[slot], partner)
+
+    to_twin = remote(shard(me), shard(me), hist_send.at[0], hist_recv.at[0], twin)
+    loads[1].wait()
+    to_twin.start()
+
+    @pl.loop(1, quads)
+    def _(k):
+        hop(me, k, k).start()
 
     halo_far(0).start()
-    halo_far(1).start()
-    first.start()
+    fwd_copy(0).start()
     halo_near.start()
 
     blocks = count * row_blocks
@@ -208,7 +217,16 @@
             hot = jnp.where(hot, 1.0, 0.0).astype(BF16)
             band[at, hbase + h : hbase + h + hstep] = mm(wts, hot, NT).astype(BF16)
 
-    for load in loads[1:]:
+    to_twin.wait_recv()
+
+    @pl.loop(1, quads)
+    def _(k):
+        hop(twin, k, quads + k).start()
+
+    halo_far(1).start()
+    fwd_copy(quads).start()
+    loads[0:2] = []
+    for load in loads:
         load.wait()
     code_copy.wait()
 
@@ -225,48 +243,49 @@
         degree = 1.0 + jnp.sum(total, axis=1, keepdims=True)
         rdeg[at, :] = jnp.broadcast_to(1.0 / degree, (tile, feat))
 
-    @pl.loop(1, pairs)
-    def _(k):
-        hist_copy(k).wait_recv()
+    @pl.loop(1, quads)
+    def _(k):
+        hop(me, k, k).wait_recv()
         fwd_copy(k).start()
+
+    @pl.loop(1, quads)
+    def _(k):
+        hop(twin, k, quads + k).wait_recv()
+        fwd_copy(quads + k).start()
 
     @pl.loop(0, rows // step)
     def _(r):
         at = pl.ds(pl.multiple_of(r * step, step), step)
         own = ext[pl.ds(pl.multiple_of(rows + r * step, step), step), :]
         base[at, :] = mm(band[at, rows : 2 * rows], ext[rows : 2 * rows, :], NN)
+        x_t[:, at] = own.T
         pre_s[at, :] = mm(own, ws_ref[...], NN) + bias_ref[...]
 
+    near_at = pl.ds(pl.multiple_of(near_here, rows), rows)
+    far_half = [pl.ds(pl.multiple_of(far_here + j * half, half), half) for j in range(2)]
     halo_near.wait_recv()
-    first.wait_recv()
-
-    @pl.loop(1, pairs)
-    def _(k):
-        fwd_copy(k).wait_recv()
-
-    near_at = pl.ds(pl.multiple_of(near_here, rows), rows)
-    far_at = pl.ds(pl.multiple_of(far_here, rows), rows)
-    far_half = [pl.ds(pl.multiple_of(far_here + j * half, half), half) for j in range(2)]
+    halo_far(0).wait_recv()
 
     @pl.loop(0, rows // step)
     def _(r):
         at = pl.ds(pl.multiple_of(r * step, step), step)
-        base[at, :] += mm(band[at, hbase:], ext[hbase:, :], NN) + mm(
-            band[at, near_at], ext[near_at, :], NN
+        base[at, :] += mm(band[at, near_at], ext[near_at, :], NN) + mm(
+            band[at, far_half[0]], ext[far_half[0], :], NN
         )
 
-    halo_far(0).wait_recv()
+    @pl.loop(0, pairs)
+    def _(k):
+        fwd_copy(k).wait_recv()
 
     @pl.loop(0, rows // step)
     def _(r):
         at = pl.ds(pl.multiple_of(r * step, step), step)
-        base[at, :] += mm(band[at, far_half[0]], ext[far_half[0], :], NN)
+        base[at, :] += mm(band[at, hbase:], ext[hbase:, :], NN)
 
     halo_far(1).wait_recv()
 
-    @pl.loop(0, rows // step)
-    def _(r):
-        at = pl.ds(pl.multiple_of(r * step, step), step)
+    for r in range(rows // step):
+        at = pl.ds(r * step, step)
         num = base[at, :] + mm(band[at, far_half[1]], ext[far_half[1], :], NN)
         recip = rdeg[at, :]
         agg = (num * recip).astype(BF16)
@@ -274,18 +293,22 @@
         sig = jax.nn.sigmoid(pre)
         hid_ref[at, :] = (pre * sig).astype(BF16)
         dz = (og_ref[at, :].astype(F32) * sig * (1.0 + pre * (1.0 - sig))).astype(BF16)
-        scaled = mm(dz, wn_ref[...], NT) * recip
-        agg_s[at, :] = agg
+        scaled = (mm(dz, wn_ref[...], NT) * recip).astype(BF16)
         dz_s[at, :] = dz
-        scaled_t[:, at] = scaled.T.astype(BF16)
-
+        scaled_t[:, at] = scaled.T
+        agg_t[:, at] = agg.T
+
+    def back_far(j):
+        return remote(out_far.at[j], in_far.at[j], back_send.at[j], back_recv.at[j], far)
+
+    back_near = remote(out_near, in_near, back_send.at[2], back_recv.at[2], partner)
     dz = dz_s[...]
     bias_sum = jnp.sum(dz.astype(F32), axis=0, keepdims=True)
     row = lax.broadcasted_iota(jnp.int32, (16, 128), 0)
     bias_rows = jnp.where(
         row == 0, bias_sum[:, :128], jnp.where(row == 1, bias_sum[:, 128:], 0.0)
     ).astype(BF16)
-    grads = (mm(ext[rows : 2 * rows, :], dz, TN), mm(agg_s[...], dz, TN))
+    grads = (mm(x_t[...], dz, NN), mm(agg_t[...], dz, NN))
     for j in range(count):
         quarter, start = divmod(j * chunk, feat)
         lanes = (quarter % 2) * 128
@@ -296,10 +319,8 @@
     pair_copy = remote(gsend.at[1 - side], gpair, pair_sem.at[0], pair_sem.at[1], partner)
     pair_copy.start()
 
-    back_far = remote(out_far, in_far, back_send.at[0], back_recv.at[0], far)
-    back_near = remote(out_near, in_near, back_send.at[1], back_recv.at[1], partner)
-    out_far[...] = mm(scaled_t[...], band[:, far_at], NN).astype(BF16)
-    back_far.start()
+    for j in range(2):
+        out_far[j] = mm(scaled_t[...], band[:, far_half[j]], NN).astype(BF16)
 
     chip = me // 2
 
@@ -323,14 +344,11 @@
     def _(k):
         rs_copy(k).start()
 
+    back_far(0).start()
+
     out_near[...] = mm(scaled_t[...], band[:, near_at], NN).astype(BF16)
     back_near.start()
-    own_t[...] = mm(scaled_t[...], band[:, rows : 2 * rows], NN)
-
-    @pl.loop(0, rows // step)
-    def _(r):
-        at = pl.ds(pl.multiple_of(r * step, step), step)
-        base[at, :] = mm(dz_s[at, :], ws_ref[...], NT)
+    own_t[...] = mm(scaled_t[...], band[:, rows : 2 * rows], NN) + mm(ws_ref[...], dz, NT)
 
     @pl.loop(1, pairs)
     def _(k):
@@ -348,6 +366,8 @@
     def _(k):
         ag_copy(k).start()
 
+    back_far(1).start()
+
     brow[...] = total[chunk:] * inv_scale
     gbias_ref[...] = brow[0:2, :]
 
@@ -357,13 +377,13 @@
         agf_copy(k).start()
 
     back_near.wait_recv()
-    back_far.wait_recv()
-
-    @pl.loop(0, rows // step)
-    def _(r):
-        at = pl.ds(pl.multiple_of(r * step, step), step)
-        spread = own_t[:, at] + in_near[:, at].astype(F32) + in_far[:, at].astype(F32)
-        feat_ref[at, :] = (base[at, :] + spread.T).astype(BF16)
+    for j in range(2):
+        back_far(j).wait_recv()
+        for r in range(half // step):
+            at = pl.ds(j * half + r * step, step)
+            late = in_far[j, :, r * step : (r + 1) * step].astype(F32)
+            spread = own_t[:, at] + in_near[:, at].astype(F32) + late
+            feat_ref[at, :] = spread.astype(BF16).T
 
     agf_first.wait_recv()
 
@@ -377,19 +397,27 @@
         out = gself_ref if quarter < 2 else gneigh_ref
         out[start : start + chunk, lanes : lanes + 128] = gfin[j].astype(F32)
 
-    first.wait_send()
+    to_twin.wait_send()
     halo_far(0).wait_send()
     halo_far(1).wait_send()
     halo_near.wait_send()
-    back_far.wait_send()
+    back_far(0).wait_send()
+    back_far(1).wait_send()
     back_near.wait_send()
     pair_copy.wait_send()
     agf_first.wait_send()
 
-    @pl.loop(1, pairs)
-    def _(k):
-        hist_copy(k).wait_send()
+    @pl.loop(1, quads)
+    def _(k):
+        hop(me, k, k).wait_send()
+        hop(twin, k, quads + k).wait_send()
+
+    @pl.loop(0, pairs)
+    def _(k):
         fwd_copy(k).wait_send()
+
+    @pl.loop(1, pairs)
+    def _(k):
         rs_copy(k).wait_send()
         ag_copy(k).wait_send()
         agf_copy(k).wait_send()
@@ -455,12 +483,13 @@
             pltpu.VMEM((rows, feat), F32),
             pltpu.VMEM((rows, feat), F32),
             pltpu.VMEM((rows, feat), BF16),
-            pltpu.VMEM((rows, feat), BF16),
-            pltpu.VMEM((feat, rows), BF16),
-            pltpu.VMEM((feat, rows), F32),
             pltpu.VMEM((feat, rows), BF16),
             pltpu.VMEM((feat, rows), BF16),
             pltpu.VMEM((feat, rows), BF16),
+            pltpu.VMEM((feat, rows), F32),
+            pltpu.VMEM((2, feat, rows // 2), BF16),
+            pltpu.VMEM((feat, rows), BF16),
+            pltpu.VMEM((2, feat, rows // 2), BF16),
             pltpu.VMEM((feat, rows), BF16),
             pltpu.VMEM((2, pairs, chunk + 16, 128), BF16),
             pltpu.VMEM((pairs, chunk + 16, 128), BF16),
@@ -473,8 +502,8 @@
             dma((8,)),
             dma((3,)),
             dma((3,)),
-            dma((2,)),
-            dma((2,)),
+            dma((3,)),
+            dma((3,)),
             dma((pairs,)),
             dma((pairs,)),
             dma((pairs,)),

time: 50.5 us -> 47 us (0.931)
  Pallas kernels: 49.7 us -> 46.2 us
    pallas_call x1, Pallas kernels: 47.4 us -> 43.9 us  [body(): pl.pallas_call(functools.partial(layer_kernel, count), out_shape=(jax.Sha...]
where the time goes in v3:
time: 47 us; the launch traced here: 46.8 us
  Pallas kernels  46.2 us (98%)
  between operations  0.64 us (1%)
    pallas_call x1, Pallas kernels, body(): pl.pallas_call(functools.partial(layer_kernel, count), out_shape=(jax.Sha...  43.9 us
    pallas_call x1, Pallas kernels, body(): pl.pallas_call(functools.partial(hand_over, 5), out_shape=tuple((jax.Shap...  2.27 us

profile of v3, /device:TPU:0, one launch (start us, length us, event | category | flops | bytes accessed | tf_op | source)
XLA Modules:
  0.0 46.8 jit_solution(15557367976815509948)
XLA Ops:
  0.6 43.9 %shard_map.146 = (bf16[1024,256]{1,0:T(8,128)(2,1)}, bf16[1024,256]{1,0:T(8,128)(2,1)}, f32[256,256]{1,0:T(8,128)}, f32[256,256]{1,0:T(8,128)}, f32[2,128]{1,0:T(2,128)}) custom-call(s32[8]{0:T(128)} %live_ref.1, s32[8,24]{1,0:T(8,128)} %cols_ref.1, s32[8,128]{1,0:T(8,128)} %ids_ref.1, f32[1,256]{1,0:T(1,128)} %bitcast.2, bf16[1024,128]{1,0:T(8,128)(2,1)} %wts_hbm.1, ...), custom_call_target="tpu_custom_call" | custom-call | tf_op jit(solution)/shard_map/pallas_call | solution.py:463
  44.6 2.3 %shard_map.147 = (bf16[1024,256]{1,0:T(8,128)(2,1)}, bf16[1024,256]{1,0:T(8,128)(2,1)}, f32[256,256]{1,0:T(8,128)}, f32[256,256]{1,0:T(8,128)}, f32[2,128]{1,0:T(2,128)}) custom-call(bf16[1024,256]{1,0:T(8,128)(2,1)} %get-tuple-element.15.refs_0_, bf16[1024,256]{1,0:T(8,128)(2,1)} %get-tuple-element.16.refs_1_, f32[256,256]{1,0:T(8,128)} %get-tuple-element.17.refs_2_, ...), custom_call_target="tpu_custom_call" | custom-call | tf_op jit(solution)/shard_map/pallas_call | solution.py:535
